TPU v7x, 256 devices: a whole 4x4x8 slice. The times are simulated.
256 devices in a mesh: row: 16 (over z, core), col: 16 (over x, y).
Axes of the slice: x: 4, y: 4, z: 8, core: 2. Of those that a mesh axis runs over, the one named last changes fastest.
Arguments:
- source: bfloat16 [262144, 128], P('row'), may hold values from -36 to 36
- target: bfloat16 [131072, 128], P('col'), may hold values from -36 to 36
- log_source: float32 [262144], P('row'), may hold values from -2 to 2
- log_target: float32 [131072], P('col'), may hold values from -2 to 2
- support: int32 [1024, 16], P('row', 'col'), may hold values from 0 to 511, as said below
- counts: int32 [1024, 16], P('row', 'col'), may hold values from 0 to 1, as said below
Outputs:
- potential_row: float32 [262144], P('row')
- potential_col: float32 [131072], P('col')
Inputs may be any that keep to these rules, and one draw needn't show every extreme that they name: `support`: slots 1 * d to 1 * d + 1 - 1 of a row block name column blocks d * 32 to (d + 1) * 32 - 1 of column device d; the live ones among them are distinct. Every column block is named by a live slot of some row block. `counts`: every row block has a live slot. In every draw each column device d has a row block whose slot d is live.
All inputs are finite; a program needn't handle non-finite values.
Results may differ from a plain program's by a relative error of at most 0.012.
Values sent between devices are 32-bit elements; how exact they have to be, the bound alone decides.
A program may use at most 64 MiB of HBM per device.

v0:
```python
import jax
import jax.numpy as jnp
from jax import lax
from jax.sharding import PartitionSpec as P

BS = 256
ITERS = 2


entropic = 0.1
floor_value = -1e30


def merged(array, axis, combine):
    everything = jax.tree.map(lambda part: lax.all_gather(part, axis), array)
    initial = jax.tree.map(lambda part: part[0], everything)

    def hop(k, so_far):
        return combine(so_far, jax.tree.map(lambda part: part[k], everything))

    return lax.fori_loop(1, lax.axis_size(axis), hop, initial)


def combine_pairs(former, latter):
    peak = jnp.maximum(former[0], latter[0])
    return (peak, former[1] * jnp.exp(former[0] - peak) + latter[1] * jnp.exp(latter[0] - peak))


def on_device(source, target, log_source, log_target, support, counts):
    row_count = support.shape[0]
    embed_width = source.shape[1]
    col_count = target.shape[0] // BS
    first_block = lax.axis_index("col") * col_count
    local_block = support - first_block
    live_slot = lax.broadcasted_iota(jnp.int32, support.shape, 1) < counts
    source_blocks = source.reshape(row_count, BS, embed_width)
    target_blocks = target.reshape(col_count, BS, embed_width)
    row_norms = jnp.sum(jnp.square(source_blocks.astype(jnp.float32)), axis=-1)
    col_norms = jnp.sum(jnp.square(target_blocks.astype(jnp.float32)), axis=-1)
    picked = target_blocks[local_block]
    products = jnp.einsum(
        "rbe,rkce->rkbc", source_blocks, picked, preferred_element_type=jnp.float32
    )
    cost_tiles = (
        (row_norms[:, None, :, None] + col_norms[local_block][:, :, None, :] - 2.0 * products)
        / embed_width
    ).astype(jnp.bfloat16)
    mask_tiles = live_slot[:, :, None, None]
    local_flat = local_block.reshape(-1)
    hit_table = (
        local_flat[:, None] == jnp.arange(col_count, dtype=jnp.int32)[None, :]
    ) & live_slot.reshape(-1)[:, None]
    hit_float = hit_table.astype(jnp.float32)
    row_weights = log_source.reshape(row_count, BS)
    col_weights = log_target.reshape(col_count, BS)
    potential_col = jnp.zeros((col_count, BS), jnp.float32)
    potential_row = jnp.zeros((row_count, BS), jnp.float32)
    for iteration in range(ITERS):
        picked_pot = potential_col[local_block]
        scores = (picked_pot[:, :, None, :] - cost_tiles.astype(jnp.float32)) / entropic
        scores = jnp.where(mask_tiles, scores, floor_value)
        local_peak = jnp.max(scores, axis=(1, 3))
        local_sum = jnp.sum(
            jnp.where(mask_tiles, jnp.exp(scores - local_peak[:, None, :, None]), 0.0), axis=(1, 3)
        )
        peak, summed = merged((local_peak, local_sum), "col", combine_pairs)
        potential_row = entropic * row_weights - entropic * (peak + jnp.log(summed))
        col_scores = (potential_row[:, None, :, None] - cost_tiles.astype(jnp.float32)) / entropic
        block_peak = jnp.max(col_scores, axis=2)
        block_sum = jnp.sum(jnp.exp(col_scores - block_peak[:, :, None, :]), axis=2)
        block_peak = jnp.where(live_slot[:, :, None], block_peak, floor_value).reshape(-1, BS)
        block_sum = jnp.where(live_slot[:, :, None], block_sum, 0.0).reshape(-1, BS)
        col_peak = jnp.max(
            jnp.where(hit_table[:, :, None], block_peak[:, None, :], floor_value), axis=0
        )
        scaled = block_sum * jnp.exp(block_peak - col_peak[local_flat])
        partial_sums = jnp.einsum("nc,nb->cb", hit_float, scaled, precision=lax.Precision.HIGHEST)
        peak, summed = merged((col_peak, partial_sums), "row", combine_pairs)
        potential_col = entropic * col_weights - entropic * (peak + jnp.log(summed))
    return (potential_row.reshape(-1), potential_col.reshape(-1))


def solution(mesh):
    placed = (P("row", None), P("col", None), P("row"), P("col"), P("row", "col"), P("row", "col"))
    return jax.shard_map(
        on_device, mesh=mesh, in_specs=placed, out_specs=(P("row"), P("col")), check_vma=False
    )
```

profile of v0, /device:TPU:1, one launch (start us, length us, event | category | flops | bytes accessed | tf_op | source)
XLA Modules:
  0.0 391.6 jit_solution(1324979493839723594)
XLA Ops:
  8.5 2.7 multiply_reduce_fusion.1
  12.0 4.7 %gather_fusion.2 = bf16[64,256,128]{2,1,0:T(8,128)(2,1)} fusion(bf16[32,256,128]{2,1,0:T(8,128)(2,1)} %bitcast.87, s32[1024]{0:T(1024)S(1)} %pad_clamp_fusion), kind=kCustom, calls=%fused_computation.2 | custom fusion | bytes 8388864 | tf_op jit(solution)/shard_map/gather | solution.py:40
  17.3 3.9 %multiply_reduce_fusion = f32[16384]{0:T(1024)S(1)} fusion(bf16[16384,128]{1,0:T(8,128)(2,1)} %param.14), kind=kLoop, calls=%fused_computation.57 | loop fusion | flops 6275072 | bytes 4259840 | tf_op jit(solution)/shard_map/reduce_sum | solution.py:38
  21.2 9.5 %fusion.11 = (f32[64,256]{1,0:T(8,128)S(1)}, bf16[64,1,256,256]{2,3,0,1:T(8,128)(2,1)}) fusion(f32[64,256]{1,0:T(8,128)S(1)} %gather_fusion, pred[64]{0:T(512)(128)(4,1)S(1)} %compare_bitcast_fusion, bf16[64,256,128]{2,1,0:T(8,128)(2,1)} %gather_fusion.2, bf16[64,256,128]{2,1,0:T(8,128)(2,1)} %bitcast.88, f32[64,256]{1,0:T(8,128)S(1)} %gather_fusion.1, ...), kind=kOutput, calls=%fused_computation.33 | convolution fusion | flops 1115668480 | bytes 17039424 | tf_op jit(solution)/shard_map/rbe,rkce->rkbc/dot_general | solution.py:41
  30.7 8.4 %fusion.14 = f32[64,256]{1,0:T(8,128)} fusion(bf16[64,1,256,256]{2,3,0,1:T(8,128)(2,1)} %get-tuple-element.593, f32[64,256]{1,0:T(8,128)S(1)} %gather_fusion, f32[64,256]{1,0:T(8,128)S(1)} %get-tuple-element.592, pred[64]{0:T(512)(128)(4,1)S(1)} %compare_bitcast_fusion), kind=kLoop, calls=%fused_computation.36 | loop fusion | flops 29343744 | bytes 8585280 | tf_op jit(solution)/shard_map/reduce_sum | solution.py:63
  40.1 49.3 %all-gather.15.cloned.1.call-done = f32[1024,256]{1,0:T(8,128)} async-done(((f32[64,256]{1,0:T(8,128)}), f32[1024,256]{1,0:T(8,128)}) %all-gather.15.cloned.1.call-update) | async-done | bytes 1048592 | tf_op jit(solution)/shard_map/all_gather | solution.py:15
  90.2 49.2 %all-gather.13.cloned.1.call-done = f32[1024,256]{1,0:T(8,128)} async-done(((f32[64,256]{1,0:T(8,128)}), f32[1024,256]{1,0:T(8,128)}) %all-gather.13.cloned.1.call-update) | async-done | bytes 1048592 | tf_op jit(solution)/shard_map/all_gather | solution.py:15
  140.3 14.4 %while.68 = (s32[]{:T(128)}, f32[64,256]{1,0:T(8,128)S(1)}, f32[64,256]{1,0:T(8,128)S(1)}, f32[16,64,256]{2,1,0:T(8,128)}, f32[16,64,256]{2,1,0:T(8,128)}, /*index=5*/s32[]{:T(128)}, s32[]{:T(128)}, s32[]{:T(128)}) while((s32[]{:T(128)}, f32[64,256]{1,0:T(8,128)S(1)}, f32[64,256]{1,0:T(8,128)S(1)}, f32[16,64,256]{2,1,0:T(8,128)}, ...), condition=%wide.region_5.6_spmd, body=%wide.region_4.5_spmd.sunk | while | flops 98309 | bytes 393347 | solution.py:21
  141.2 0.9 fusion.60
  142.2 0.9 fusion.60
  143.1 0.9 fusion.60
  154.7 5.7 %fusion.17 = f32[64,256]{1,0:T(8,128)S(1)} fusion(bf16[64,1,256,256]{2,3,0,1:T(8,128)(2,1)} %get-tuple-element.593, f32[64,256]{1,0:T(8,128)S(1)} %multiply_subtract_fusion.1), kind=kLoop, calls=%fused_computation.39 | loop fusion | flops 16760832 | bytes 8519680 | tf_op jit(solution)/shard_map/reduce_max | solution.py:69
  160.4 7.5 %fusion.19 = f32[64,256]{1,0:T(8,128)S(1)} fusion(bf16[64,1,256,256]{2,3,0,1:T(8,128)(2,1)} %get-tuple-element.593, f32[64,256]{1,0:T(8,128)S(1)} %fusion.17, f32[64,256]{1,0:T(8,128)S(1)} %multiply_subtract_fusion.1), kind=kLoop, calls=%fused_computation.41 | loop fusion | flops 20955136 | bytes 8585216 | tf_op jit(solution)/shard_map/reduce_sum | solution.py:70
  169.0 20.8 %all-gather.2 = f32[512,256]{1,0:T(8,128)S(1)} all-gather(f32[32,256]{1,0:T(8,128)S(1)} %select_reduce_fusion.1), channel_id=4, replica_groups=mesh['row'=16,'col'=16] {'row'}, dimensions={0}, use_global_device_ids=true | all-gather | bytes 557056 | tf_op jit(solution)/shard_map/all_gather | solution.py:15
  190.1 16.6 %all-gather.3 = f32[512,256]{1,0:T(8,128)S(1)} all-gather(f32[32,256]{1,0:T(8,128)S(1)} %fusion.39), channel_id=5, replica_groups=mesh['row'=16,'col'=16] {'row'}, dimensions={0}, use_global_device_ids=true | all-gather | bytes 557056 | tf_op jit(solution)/shard_map/all_gather | solution.py:15
  208.3 6.1 %fusion.23 = f32[64,256]{1,0:T(8,128)S(1)} fusion(bf16[64,1,256,256]{2,3,0,1:T(8,128)(2,1)} %get-tuple-element.593, f32[64,256]{1,0:T(8,128)S(1)} %gather_fusion.4, pred[64]{0:T(512)(128)(4,1)S(1)} %compare_bitcast_fusion), kind=kLoop, calls=%fused_computation.45 | loop fusion | flops 20955136 | bytes 8519744 | tf_op jit(solution)/shard_map/reduce_max | solution.py:62
  214.4 8.3 %fusion.26 = f32[64,256]{1,0:T(8,128)} fusion(bf16[64,1,256,256]{2,3,0,1:T(8,128)(2,1)} %get-tuple-element.593, f32[64,256]{1,0:T(8,128)S(1)} %gather_fusion.4, f32[64,256]{1,0:T(8,128)S(1)} %fusion.23, pred[64]{0:T(512)(128)(4,1)S(1)} %compare_bitcast_fusion), kind=kLoop, calls=%fused_computation.48 | loop fusion | flops 29343744 | bytes 8585280 | tf_op jit(solution)/shard_map/reduce_sum | solution.py:63
  223.3 42.5 %all-gather.19.cloned.1.call-done = f32[1024,256]{1,0:T(8,128)} async-done(((f32[64,256]{1,0:T(8,128)}), f32[1024,256]{1,0:T(8,128)}) %all-gather.19.cloned.1.call-update) | async-done | bytes 1048592 | tf_op jit(solution)/shard_map/all_gather | solution.py:15
  266.7 49.1 %all-gather.17.cloned.1.call-done = f32[1024,256]{1,0:T(8,128)} async-done(((f32[64,256]{1,0:T(8,128)}), f32[1024,256]{1,0:T(8,128)}) %all-gather.17.cloned.1.call-update) | async-done | bytes 1048592 | tf_op jit(solution)/shard_map/all_gather | solution.py:15
  316.6 14.4 %while.70 = (s32[]{:T(128)}, f32[64,256]{1,0:T(8,128)S(1)}, f32[64,256]{1,0:T(8,128)S(1)}, f32[16,64,256]{2,1,0:T(8,128)}, f32[16,64,256]{2,1,0:T(8,128)}, /*index=5*/s32[]{:T(128)}, s32[]{:T(128)}, s32[]{:T(128)}) while((s32[]{:T(128)}, f32[64,256]{1,0:T(8,128)S(1)}, f32[64,256]{1,0:T(8,128)S(1)}, f32[16,64,256]{2,1,0:T(8,128)}, ...), condition=%wide.region_14.15_spmd, body=%wide.region_13.14_spmd.sunk | while | flops 98309 | bytes 393347 | solution.py:21
  331.0 5.7 %fusion.29 = f32[64,256]{1,0:T(8,128)S(1)} fusion(bf16[64,1,256,256]{2,3,0,1:T(8,128)(2,1)} %get-tuple-element.593, f32[64,256]{1,0:T(8,128)S(1)} %multiply_subtract_fusion), kind=kLoop, calls=%fused_computation.51 | loop fusion | flops 16760832 | bytes 8519680 | tf_op jit(solution)/shard_map/reduce_max | solution.py:69
  336.7 7.5 %fusion.31 = f32[64,256]{1,0:T(8,128)S(1)} fusion(bf16[64,1,256,256]{2,3,0,1:T(8,128)(2,1)} %get-tuple-element.593, f32[64,256]{1,0:T(8,128)S(1)} %fusion.29, f32[64,256]{1,0:T(8,128)S(1)} %multiply_subtract_fusion), kind=kLoop, calls=%fused_computation.53 | loop fusion | flops 20955136 | bytes 8585216 | tf_op jit(solution)/shard_map/reduce_sum | solution.py:70
  345.4 20.8 %all-gather.6 = f32[512,256]{1,0:T(8,128)S(1)} all-gather(f32[32,256]{1,0:T(8,128)S(1)} %select_reduce_fusion), channel_id=8, replica_groups=mesh['row'=16,'col'=16] {'row'}, dimensions={0}, use_global_device_ids=true | all-gather | bytes 557056 | tf_op jit(solution)/shard_map/all_gather | solution.py:15
  366.4 16.4 %all-gather.7 = f32[512,256]{1,0:T(8,128)S(1)} all-gather(f32[32,256]{1,0:T(8,128)S(1)} %fusion.34), channel_id=9, replica_groups=mesh['row'=16,'col'=16] {'row'}, dimensions={0}, use_global_device_ids=true | all-gather | bytes 557056 | tf_op jit(solution)/shard_map/all_gather | solution.py:15
  (111 shorter events, 40.5 us)
Async XLA Ops:
  7.2 82.2 %all-gather.15.cloned.1.call-start = ((), (), s32[]{:S(2)}) async-start(), calls=%async_computation.1 | async-start | bytes 1114112 | tf_op jit(solution)/shard_map/all_gather | solution.py:15
  30.7 8.4 %copy-start.1 = (f32[64,256]{1,0:T(8,128)}, f32[64,256]{1,0:T(8,128)S(1)}, u32[]{:S(2)}) copy-start(f32[64,256]{1,0:T(8,128)S(1)} %get-tuple-element.592) | copy-start | bytes 196612
  30.7 9.2 %copy-start.2 = (f32[16384]{0:T(1024)S(1)}, f32[16384]{0:T(1024)}, u32[]{:S(2)}) copy-start(f32[16384]{0:T(1024)} %param.16) | copy-start | bytes 196612
  30.7 9.2 %copy-start.3 = (f32[8192]{0:T(1024)S(1)}, f32[8192]{0:T(1024)}, u32[]{:S(2)}) copy-start(f32[8192]{0:T(1024)} %param.17) | copy-start | bytes 98308
  39.1 100.3 %all-gather.13.cloned.1.call-start = ((), (), s32[]{:S(2)}) async-start(), calls=%async_computation | async-start | bytes 1114112 | tf_op jit(solution)/shard_map/all_gather | solution.py:15
  39.9 226.0 %all-gather.19.cloned.1.call-start = ((), (), s32[]{:S(2)}) async-start(), calls=%async_computation.3 | async-start | bytes 1114112 | tf_op jit(solution)/shard_map/all_gather | solution.py:15
  214.4 8.4 %copy-start = (f32[64,256]{1,0:T(8,128)}, f32[64,256]{1,0:T(8,128)S(1)}, u32[]{:S(2)}) copy-start(f32[64,256]{1,0:T(8,128)S(1)} %fusion.23) | copy-start | bytes 196612
  222.8 93.0 %all-gather.17.cloned.1.call-start = ((), (), s32[]{:S(2)}) async-start(), calls=%async_computation.2 | async-start | bytes 1114112 | tf_op jit(solution)/shard_map/all_gather | solution.py:15
Sparse Core Ops, SparseCore 0:
  39.2 50.0 all-gather.14
  92.4 47.0 all-gather.12
  222.9 42.9 all-gather.18
  268.7 47.0 all-gather.16
where the time goes:
time: 394 us; the launch traced here: 392 us
  waiting for transfers between devices  191 us (48%)
  other arithmetic  87.4 us (22%)
  blocking collectives  74.7 us (19%)
  between operations  14 us (4%)
  local copies, waits for them, and re-layouts  12.7 us (3%)
  matrix products  10 us (3%)
    all_gather x4, waiting for transfers between devices, merged(): everything = jax.tree.map(lambda part: lax.all_gather(part, axis), array)  190 us
    all_gather x4, blocking collectives, merged(): everything = jax.tree.map(lambda part: lax.all_gather(part, axis), array)  74.7 us
    add x60, other arithmetic, combine_pairs(): former[1] * jnp.exp(former[0] - peak)  29.1 us
    reduce_sum x2, other arithmetic, on_device(): jnp.sum(jnp.where(mask_tiles, jnp.exp(scores - local_peak[:, None, :, Non...  16.7 us
    reduce_sum x2, other arithmetic, on_device(): block_sum = jnp.sum(jnp.exp(col_scores - block_peak[:, :, None, :]), axis=2)  14.9 us
    reduce_max x2, other arithmetic, on_device(): block_peak = jnp.max(col_scores, axis=2)  11.4 us
    dot_general x1, matrix products, on_device(): jnp.einsum('rbe,rkce->rkbc', source_blocks, picked, preferred_element_typ...  9.48 us
  transfers between devices with their start and end apart: 4, of which 4 were waited for; matrix products, arithmetic and copies ran while one was open for 0% of the time, Pallas kernels for 0%

commit v1 on v0

v1 whole, which is shorter than its diff:
```python
import functools
import math

import jax
import jax.numpy as jnp
from jax import lax
from jax.experimental import pallas as pl
from jax.experimental.pallas import tpu as pltpu
from jax.sharding import PartitionSpec as P

BS = 256
ITERS = 2
entropic = 0.1
floor_value = -1e30
LOG2E = math.log2(math.e)
SCALE = LOG2E / entropic
MESH = pl.DeviceIdType.MESH
GROUP = 4


def dot_nt(a, b):
    return lax.dot_general(a, b, (((1,), (1,)), ((), ())), preferred_element_type=jnp.float32)


def lane_column(row):
    return jnp.transpose(jnp.broadcast_to(row, (128, 128)))


def partial_lse(scores):
    stacked = scores.reshape(BS // 8, 8, 128)
    peak = jnp.max(stacked, axis=0)
    return peak + LOG2E * jnp.log(jnp.sum(jnp.exp2(stacked - peak[None]), axis=0))


def stacked_lse(parts):
    peak = functools.reduce(jnp.maximum, parts)
    total = functools.reduce(jnp.add, [jnp.exp2(part - peak) for part in parts])
    return peak + LOG2E * jnp.log(total)


def kernel(
    n_row, n_col,
    sup, cnt, src_hbm, tgt_hbm, ls, lt,
    f_out, g_out,
    src, tgt, dots_qp, dots_pq, gcol, fcol, part8, part16, key,
    lrow, rs_row, fall, lcol, lpart, rs_col, gall, rnorm, cnorm,
    tgt_sem, src_sem,
    rs_row_send, rs_row_recv, ag_row_send, ag_row_recv,
    rs_col_send, rs_col_recv, ag_col_send, ag_col_recv,
):
    row_count = src.shape[0]
    col_count = tgt.shape[0]
    embed = src.shape[2]
    my_row, my_col = lax.axis_index("row"), lax.axis_index("col")
    first_block = my_col * col_count
    dot_scale = 2.0 * SCALE / embed

    tgt_copy = pltpu.make_async_copy(tgt_hbm, tgt, tgt_sem)
    tgt_copy.start()

    def src_copy(c):
        here = pl.ds(c * GROUP, GROUP)
        return pltpu.make_async_copy(src_hbm.at[here], src.at[here], src_sem.at[c])

    for c in range(n_col):
        src_copy(c).start()

    barrier = pltpu.get_barrier_semaphore()
    for o in range(1, n_col):
        pl.semaphore_signal(barrier, inc=1, device_id=(my_row, lax.rem(my_col + o, n_col)), device_id_type=MESH)
    for o in range(1, n_row):
        pl.semaphore_signal(barrier, inc=1, device_id=(lax.rem(my_row + o, n_row), my_col), device_id_type=MESH)

    def block_of(i):
        return jnp.clip(sup[i, 0] - first_block, 0, col_count - 1)

    tgt_copy.wait()

    @pl.loop(0, n_row)
    def _(o):
        for a in range(2):
            block = tgt[2 * o + a].astype(jnp.float32)
            square = block * block
            high = square.astype(jnp.bfloat16)
            low = (square - high.astype(jnp.float32)).astype(jnp.bfloat16)
            ones = jnp.ones((8, embed), jnp.bfloat16)
            across = (dot_nt(ones, high) + dot_nt(ones, low)) * (1.0 / embed)
            for h in range(2):
                cnorm[o, pl.ds(2 * a + h, 1), :] = across[0:1, h * 128:(h + 1) * 128]
            down = jnp.sum(square, axis=1, keepdims=True) * (-SCALE / embed)
            gcol[2 * o + a] = jnp.broadcast_to(down, (BS, 128))

    pl.semaphore_wait(barrier, n_row + n_col - 2)

    def rs_row_copy(it, c):
        return pltpu.make_async_remote_copy(
            src_ref=lrow.at[it, c], dst_ref=rs_row.at[it, my_col],
            send_sem=rs_row_send.at[it, c], recv_sem=rs_row_recv.at[it, my_col],
            device_id=(my_row, c), device_id_type=MESH)

    def ag_row_copy(it, peer):
        return pltpu.make_async_remote_copy(
            src_ref=fall.at[it, my_col], dst_ref=fall.at[it, my_col],
            send_sem=ag_row_send.at[it, peer], recv_sem=ag_row_recv.at[it, my_col],
            device_id=(my_row, peer), device_id_type=MESH)

    def rs_col_copy(it, r):
        return pltpu.make_async_remote_copy(
            src_ref=lcol.at[it, r], dst_ref=rs_col.at[it, my_row],
            send_sem=rs_col_send.at[it, r], recv_sem=rs_col_recv.at[it, my_row],
            device_id=(r, my_col), device_id_type=MESH)

    def ag_col_copy(it, peer):
        return pltpu.make_async_remote_copy(
            src_ref=gall.at[it, my_row], dst_ref=gall.at[it, my_row],
            send_sem=ag_col_send.at[it, peer], recv_sem=ag_col_recv.at[it, my_row],
            device_id=(peer, my_col), device_id_type=MESH)

    def arrived(buffer, sem, it, slot):
        pltpu.make_async_copy(buffer.at[it, slot], buffer.at[it, slot], sem.at[it, slot]).wait()

    def row_chunk(it, c):
        for t in range(GROUP):
            i = GROUP * c + t
            block = block_of(i)
            dead = jnp.where(cnt[i, 0] > 0, 0.0, floor_value)
            if it == 0:
                dots_qp[i] = dot_nt(tgt[block], src[i]) * dot_scale
            for h in range(2):
                scores = dots_qp[i, :, h * 128:(h + 1) * 128] + gcol[block]
                part8[pl.ds(8 * (2 * t + h), 8), :] = partial_lse(scores) + dead
        lrow[it, c] = stacked_lse([part8[pl.ds(s, 8, stride=8), :] for s in range(8)])

        @pl.when(c != my_col)
        def _():
            rs_row_copy(it, c).start()

        @pl.when(c == my_col)
        def _():
            rs_row[it, my_col] = lrow[it, c]

    def row_owner(it):
        for o in range(1, n_col):
            arrived(rs_row, rs_row_recv, it, lax.rem(my_col + o, n_col))
        total = stacked_lse([rs_row[it, d] for d in range(n_col)])
        fall[it, my_col] = ls[my_col] * LOG2E - total
        for o in range(1, n_col):
            ag_row_copy(it, lax.rem(my_col + o, n_col)).start()

    def col_chunk(it, c):
        @pl.when(c != my_col)
        def _():
            arrived(fall, ag_row_recv, it, c)

        for t in range(GROUP):
            i = GROUP * c + t
            for h in range(2):
                fcol[h * 128:(h + 1) * 128, :] = lane_column(fall[it, c, pl.ds(2 * t + h, 1), :])
            for h in range(2):
                scores = dots_pq[i, :, h * 128:(h + 1) * 128] + fcol[...]
                part8[pl.ds(8 * (GROUP * h + t), 8), :] = partial_lse(scores)
        lpart[c] = stacked_lse([part8[pl.ds(s, 8, stride=8), :] for s in range(8)])

    def col_send(it, r):
        for a in range(2):
            mine = jnp.where(key[...] == 2 * r + a, lpart[...], floor_value)
            peak = jnp.max(mine, axis=0)
            total = jnp.sum(jnp.exp2(mine - peak[None]), axis=0)
            part16[pl.ds(8 * a, 8), :] = peak + LOG2E * jnp.log(total)
        lcol[it, r] = stacked_lse([part16[pl.ds(s, 4, stride=4), :] for s in range(4)])

        @pl.when(r != my_row)
        def _():
            rs_col_copy(it, r).start()

        @pl.when(r == my_row)
        def _():
            rs_col[it, my_row] = lcol[it, r]

    def col_owner(it):
        for o in range(1, n_row):
            arrived(rs_col, rs_col_recv, it, lax.rem(my_row + o, n_row))
        total = stacked_lse([rs_col[it, d] for d in range(n_row)])
        gall[it, my_row] = lt[my_row] * LOG2E - total
        for o in range(1, n_row):
            ag_col_copy(it, lax.rem(my_row + o, n_row)).start()

    def make_chunk(c):
        sublane = lax.broadcasted_iota(jnp.int32, (8, 128), 0)
        names = jnp.full((8, 128), -1, jnp.int32)
        for t in range(GROUP):
            i = GROUP * c + t
            block = block_of(i)
            dots_pq[i] = dot_nt(src[i], tgt[block]) * dot_scale
            name = jnp.where(cnt[i, 0] > 0, block, -1)
            names = jnp.where(lax.rem(sublane, GROUP) == t, name, names)
            piece = src[i].astype(jnp.float32)
            square = piece * piece
            high = square.astype(jnp.bfloat16)
            low = (square - high.astype(jnp.float32)).astype(jnp.bfloat16)
            ones = jnp.ones((8, embed), jnp.bfloat16)
            across = (dot_nt(ones, high) + dot_nt(ones, low)) * (1.0 / embed)
            for h in range(2):
                rnorm[c, pl.ds(2 * t + h, 1), :] = across[0:1, h * 128:(h + 1) * 128]
        key[c] = names

    for it in range(ITERS):
        @pl.loop(0, n_col)
        def _(c):
            if it == 0:
                src_copy(c).wait()
            row_chunk(it, c)

        if it == 0:
            pl.loop(0, n_col)(make_chunk)
        row_owner(it)

        @pl.loop(0, n_col)
        def _(c):
            col_chunk(it, c)

        @pl.loop(0, n_row)
        def _(r):
            col_send(it, r)

        for o in range(1, n_col):
            peer = lax.rem(my_col + o, n_col)
            rs_row_copy(it, peer).wait_send()
            ag_row_copy(it, peer).wait_send()
        col_owner(it)
        if it == ITERS - 1:
            f_out[...] = fall[it] * (1.0 / SCALE) + rnorm[...]

        @pl.loop(0, n_row)
        def _(r):
            @pl.when(r != my_row)
            def _():
                arrived(gall, ag_col_recv, it, r)

            if it < ITERS - 1:
                for a in range(2):
                    for h in range(2):
                        gcol[2 * r + a, h * 128:(h + 1) * 128, :] = lane_column(gall[it, r, pl.ds(2 * a + h, 1), :])

        for o in range(1, n_row):
            peer = lax.rem(my_row + o, n_row)
            rs_col_copy(it, peer).wait_send()
            ag_col_copy(it, peer).wait_send()
    g_out[...] = gall[ITERS - 1] * (1.0 / SCALE) + cnorm[...]


def on_device(n_row, n_col, source, target, log_source, log_target, support, counts):
    row_count = support.shape[0]
    embed = source.shape[1]
    col_count = target.shape[0] // BS
    f32 = jnp.float32
    smem = pl.BlockSpec(memory_space=pltpu.SMEM)
    vmem = pl.BlockSpec(memory_space=pltpu.VMEM)
    hbm = pl.BlockSpec(memory_space=pl.ANY)
    dma = pltpu.SemaphoreType.DMA
    row_shape, col_shape = (n_col, 8, 128), (n_row, 4, 128)
    f, g = pl.pallas_call(
        functools.partial(kernel, n_row, n_col),
        out_shape=(jax.ShapeDtypeStruct(row_shape, f32), jax.ShapeDtypeStruct(col_shape, f32)),
        in_specs=[smem, smem, hbm, hbm, vmem, vmem],
        out_specs=(vmem, vmem),
        scratch_shapes=[
            pltpu.VMEM((row_count, BS, embed), jnp.bfloat16),
            pltpu.VMEM((col_count, BS, embed), jnp.bfloat16),
            pltpu.VMEM((row_count, BS, BS), f32),
            pltpu.VMEM((row_count, BS, BS), f32),
            pltpu.VMEM((col_count, BS, 128), f32),
            pltpu.VMEM((BS, 128), f32),
            pltpu.VMEM((64, 128), f32),
            pltpu.VMEM((16, 128), f32),
            pltpu.VMEM(row_shape, jnp.int32),
            pltpu.VMEM((ITERS,) + row_shape, f32),
            pltpu.VMEM((ITERS,) + row_shape, f32),
            pltpu.VMEM((ITERS,) + row_shape, f32),
            pltpu.VMEM((ITERS,) + col_shape, f32),
            pltpu.VMEM(row_shape, f32),
            pltpu.VMEM((ITERS,) + col_shape, f32),
            pltpu.VMEM((ITERS,) + col_shape, f32),
            pltpu.VMEM(row_shape, f32),
            pltpu.VMEM(col_shape, f32),
            dma(()),
            dma((n_col,)),
        ] + [dma((ITERS, n_col))] * 4 + [dma((ITERS, n_row))] * 4,
        compiler_params=pltpu.CompilerParams(
            collective_id=0, has_side_effects=True, vmem_limit_bytes=56 * 1024 * 1024),
    )(
        support, counts,
        source.reshape(row_count, BS, embed), target.reshape(col_count, BS, embed),
        log_source.reshape(row_shape), log_target.reshape(col_shape),
    )
    return f.reshape(-1), g.reshape(-1)


def solution(mesh):
    placed = (P("row", None), P("col", None), P("row"), P("col"), P("row", "col"), P("row", "col"))
    body = functools.partial(on_device, mesh.shape["row"], mesh.shape["col"])
    return jax.shard_map(
        body, mesh=mesh, in_specs=placed, out_specs=(P("row"), P("col")), check_vma=False
    )
```

time: 394 us -> 83.2 us (0.21)
  waiting for transfers between devices: 191 us -> 0 us
  other arithmetic: 87.4 us -> 0 us
  Pallas kernels: 0 us -> 76.6 us
  blocking collectives: 74.7 us -> 0 us
  between operations: 14 us -> 0.64 us
  matrix products: 10 us -> 0 us
  local copies, waits for them, and re-layouts: 12.7 us -> 5.56 us
    all_gather x4 -> x0, waiting for transfers between devices: 190 us -> none  [merged(): everything = jax.tree.map(lambda part: lax.all_gather(part, axis), array)]
    pallas_call x0 -> x1, Pallas kernels: none -> 76.6 us  [on_device(): pl.pallas_call(functools.partial(kernel, n_row, n_col), out_shape=(jax.Sh...]
    all_gather x4 -> x0, blocking collectives: 74.7 us -> none  [merged(): everything = jax.tree.map(lambda part: lax.all_gather(part, axis), array)]
    reduce_sum x6 -> x0, other arithmetic: 38.3 us -> none  [the longest x2 16.7 us: on_device(): jnp.sum(jnp.where(mask_tiles, jnp.exp(scores - local_peak[:, None, :, Non...]
    add x60 -> x0, other arithmetic: 29.1 us -> none  [combine_pairs(): former[1] * jnp.exp(former[0] - peak)]
    reduce_max x5 -> x0, other arithmetic: 18.4 us -> none  [the longest x2 11.4 us: on_device(): block_peak = jnp.max(col_scores, axis=2)]
    dot_general x3 -> x0, matrix products: 10 us -> none  [the longest x1 9.48 us: on_device(): jnp.einsum('rbe,rkce->rkbc', source_blocks, picked, preferred_element_typ...]
    gather x6 -> x0, local copies, waits for them, and re-layouts: 7.92 us -> none  [the longest x1 4.65 us: on_device(): picked = target_blocks[local_block]]
  transfers between devices with their start and end apart: 4 -> 0, of which waited for: 4 -> 0; matrix products, arithmetic and copies ran while one was open for 0% -> 0% of each run, Pallas kernels for 0% -> 0%
where the time goes in v1:
time: 83.2 us; the launch traced here: 82.8 us
  Pallas kernels  76.6 us (92%)
  local copies, waits for them, and re-layouts  5.56 us (7%)
    pallas_call x1, Pallas kernels, on_device(): pl.pallas_call(functools.partial(kernel, n_row, n_col), out_shape=(jax.Sh...  76.6 us
    unnamed x4, local copies, waits for them, and re-layouts  5.56 us

profile of v1, /device:TPU:1, one launch (start us, length us, event | category | flops | bytes accessed | tf_op | source)
XLA Modules:
  0.0 82.8 jit_solution(4014150671119671573)
XLA Ops:
  0.6 1.4 %copy.8.sup = s32[64,1]{1,0:T(8,128)} copy(s32[64,1]{0,1:T(1,128)} %param.10) | data formatting | bytes 512 | tf_op args[4]
  2.0 1.4 %copy.9.cnt = s32[64,1]{1,0:T(8,128)} copy(s32[64,1]{0,1:T(1,128)} %param.11) | data formatting | bytes 512 | tf_op args[5]
  3.3 76.6 %shard_map.77 = (f32[16,8,128]{2,1,0:T(8,128)}, f32[16,4,128]{2,1,0:T(4,128)}) custom-call(s32[64,1]{1,0:T(8,128)} %copy.8.sup, s32[64,1]{1,0:T(8,128)} %copy.9.cnt, bf16[64,256,128]{2,1,0:T(8,128)(2,1)} %bitcast.6, bf16[32,256,128]{2,1,0:T(8,128)(2,1)} %bitcast.7, f32[16,8,128]{2,1,0:T(8,128)} %bitcast.8, f32[16,4,128]{2,1,0:T(4,128)} %bitcast.10), custom_call_target="tpu_custom_call" | custom-call | tf_op jit(solution)/shard_map/pallas_call | solution.py:262
  80.0 1.5 %copy.12 = f32[16384]{0:T(1024)} copy(f32[16384]{0:T(1024)} %bitcast.9) | data formatting | bytes 131072
  81.5 1.4 %copy.13 = f32[8192]{0:T(1024)} copy(f32[8192]{0:T(1024)} %bitcast.11) | data formatting | bytes 65536

commit v2 on v0

v2 whole, which is shorter than its diff:
```python
import functools
import math

import jax
import jax.numpy as jnp
from jax import lax
from jax.experimental import pallas as pl
from jax.experimental.pallas import tpu as pltpu
from jax.sharding import PartitionSpec as P

BS = 256
ITERS = 2
entropic = 0.1
floor_value = -1e30
LOG2E = math.log2(math.e)
SCALE = LOG2E / entropic
MESH = pl.DeviceIdType.MESH
TILES = 4
GROUPS = 4
PART = 64


def dot_nt(a, b):
    return lax.dot_general(a, b, (((1,), (1,)), ((), ())), preferred_element_type=jnp.float32)


def lane_column(row):
    return jnp.transpose(jnp.broadcast_to(row, (128, 128)))


def tree(op, parts):
    parts = list(parts)
    while len(parts) > 1:
        paired = [op(a, b) for a, b in zip(parts[::2], parts[1::2])]
        parts = paired + parts[len(parts) - len(parts) % 2:]
    return parts[0]


def merged(pairs):
    peak = tree(jnp.maximum, [p for p, _ in pairs])
    return peak, tree(jnp.add, [s * jnp.exp2(p - peak) for p, s in pairs])


def log_sum(pair):
    return pair[0] + LOG2E * jnp.log(pair[1])


def merged_logs(parts):
    peak = tree(jnp.maximum, parts)
    return peak + LOG2E * jnp.log(tree(jnp.add, [jnp.exp2(part - peak) for part in parts]))


def tile_pairs(products, offsets):
    pairs = []
    for k in range(0, BS, PART):
        scores = (products(k) + offsets(k)).reshape(PART // 8, 8, 128)
        peak = jnp.max(scores, axis=0)
        pairs.append((peak, jnp.sum(jnp.exp2(scores - peak[None]), axis=0)))
    return merged(pairs)


def sublane_pairs(peaks, sums, count, stride):
    return merged([
        (peaks[pl.ds(s, count, stride=stride), :], sums[pl.ds(s, count, stride=stride), :])
        for s in range(stride)])


def squares(block):
    wide = block.astype(jnp.float32)
    return wide * wide


def norms_across(block):
    square = squares(block)
    high = square.astype(jnp.bfloat16)
    low = (square - high.astype(jnp.float32)).astype(jnp.bfloat16)
    ones = jnp.ones((8, block.shape[1]), jnp.bfloat16)
    return ((dot_nt(ones, high) + dot_nt(ones, low)) * (1.0 / block.shape[1]))[0:1]


def block_of(r, i):
    return jnp.clip(r.sup[0, i] - r.first_block, 0, r.tgt.shape[0] - 1)


def start_columns(r, o):
    for a in range(4):
        block = r.tgt[4 * o + a]
        down = jnp.sum(squares(block), axis=1, keepdims=True) * (-SCALE / block.shape[1])
        r.gcol[4 * o + a] = jnp.broadcast_to(down, (BS, 128))


def row_group(r, it, g, chunks, place):
    for k in range(chunks):
        c = chunks * g + k
        for t in range(TILES):
            i = TILES * c + t
            block = block_of(r, i)
            dead = jnp.where(r.cnt[0, i] > 0, 0.0, floor_value)
            if it == 0:
                made = dot_nt(r.tgt[block], r.src[i]) * (2.0 * SCALE / r.src.shape[2])
                r.dots_qp[i] = made
            for h in range(2):
                lanes = slice(h * 128, (h + 1) * 128)
                if it == 0:
                    products = lambda k: made[k:k + PART, lanes]
                else:
                    products = lambda k: r.dots_qp[i, k:k + PART, lanes]
                peak, total = tile_pairs(products, lambda k: r.gcol[block, k:k + PART, :])
                here = pl.ds(64 * k + 8 * (2 * t + h), 8)
                r.peaks[here, :] = peak + dead
                r.sums[here, :] = total
        at = pl.ds(64 * k, 64)
        place(c, log_sum(sublane_pairs(r.peaks.at[at], r.sums.at[at], 8, 8)))


def make_group(r, g, chunks):
    sublane = lax.broadcasted_iota(jnp.int32, (8, 128), 0)
    for k in range(chunks):
        c = chunks * g + k
        names = jnp.full((8, 128), -1, jnp.int32)
        for t in range(TILES):
            i = TILES * c + t
            block = block_of(r, i)
            r.dots_pq[i] = dot_nt(r.src[i], r.tgt[block]) * (2.0 * SCALE / r.src.shape[2])
            name = jnp.where(r.cnt[0, i] > 0, block, -1)
            names = jnp.where(lax.rem(sublane, TILES) == t, name, names)
        r.key[c] = names


def col_group(r, g, chunks):
    for k in range(chunks):
        c = chunks * g + k
        for t in range(TILES):
            i = TILES * c + t
            down = [lane_column(r.fall[c, pl.ds(2 * t + h, 1), :]) for h in range(2)]
            for h in range(2):
                peak, total = tile_pairs(
                    lambda k: r.dots_pq[i, k:k + PART, h * 128:(h + 1) * 128],
                    lambda k: down[k // 128][k % 128:k % 128 + PART])
                here = pl.ds(64 * k + 8 * (TILES * h + t), 8)
                r.peaks[here, :] = peak
                r.sums[here, :] = total
        at = pl.ds(64 * k, 64)
        r.lpart[c] = log_sum(sublane_pairs(r.peaks.at[at], r.sums.at[at], 8, 8))


def merge_columns(r, chunk):
    for u in range(4):
        mine = jnp.where(r.key[...] == 4 * chunk + u, r.lpart[...], floor_value)
        peak = jnp.max(mine, axis=0)
        here = pl.ds(8 * u, 8)
        r.peaks[here, :] = peak
        r.sums[here, :] = jnp.sum(jnp.exp2(mine - peak[None]), axis=0)
    return log_sum(sublane_pairs(r.peaks, r.sums, 8, 4))


def spread_columns(r, chunk, rows):
    for j in range(8):
        r.gcol[4 * chunk + j // 2, (j % 2) * 128:(j % 2 + 1) * 128, :] = lane_column(rows[j:j + 1])


REFS = (
    "sup", "cnt", "src_hbm", "tgt_hbm", "ls", "lt", "f_out", "g_out", "src", "tgt", "dots_qp", "dots_pq",
    "gcol", "peaks", "sums", "key", "fall", "lpart", "rnorm", "cnorm", "first", "second", "stage", "pair",
    "ring", "gall", "tgt_sem", "src_sem", "first_send", "first_recv", "second_send", "second_recv",
    "pair_send", "pair_recv", "ring_send", "ring_recv", "back_send", "back_recv",
)


class Refs:
    pass


def kernel(n_row, n_col, *refs):
    r = Refs()
    for name, ref in zip(REFS, refs, strict=True):
        setattr(r, name, ref)
    side = math.isqrt(n_col)
    depth = n_row // 2
    my_row, my_col = lax.axis_index("row"), lax.axis_index("col")
    my_x, my_y = my_col // side, lax.rem(my_col, side)
    my_z, my_core = my_row // 2, lax.rem(my_row, 2)
    other = 1 - my_core
    r.first_block = my_col * r.tgt.shape[0]
    chunks = n_col // GROUPS
    half = r.gall.shape[2]

    tgt_copy = pltpu.make_async_copy(r.tgt_hbm, r.tgt, r.tgt_sem)
    tgt_copy.start()

    def src_copy(g):
        here = pl.ds(g * chunks * TILES, chunks * TILES)
        return pltpu.make_async_copy(r.src_hbm.at[here], r.src.at[here], r.src_sem.at[g])

    for g in range(GROUPS):
        src_copy(g).start()

    def on_x(o):
        return (my_row, lax.rem(my_x + o, side) * side + my_y)

    def on_y(o):
        return (my_row, my_x * side + lax.rem(my_y + o, side))

    def on_z(o):
        return (lax.rem(my_z + o, depth) * 2 + my_core, my_col)

    sibling = (my_z * 2 + other, my_col)
    barrier = pltpu.get_barrier_semaphore()
    for o in range(1, depth):
        pl.semaphore_signal(barrier, inc=1, device_id=on_z(o), device_id_type=MESH)
    for o in range(1, side):
        pl.semaphore_signal(barrier, inc=1, device_id=on_x(o), device_id_type=MESH)
        pl.semaphore_signal(barrier, inc=1, device_id=on_y(o), device_id_type=MESH)
    pl.semaphore_signal(barrier, inc=1, device_id=sibling, device_id_type=MESH)

    def place_of(g, which):
        x_now = lax.rem(g + which, 2) == 0
        return x_now, jnp.where(x_now, my_x, my_y)

    def row_copy(it, g, which, o):
        buffer, send, recv = (r.first, r.first_send, r.first_recv) if which == 0 else (
            r.second, r.second_send, r.second_recv)
        x_now, me = place_of(g, which)
        (row, x_col), (_, y_col) = on_x(o), on_y(o)
        here = buffer.at[it, me, pl.ds(g * chunks, chunks)]
        return pltpu.make_async_remote_copy(
            src_ref=here, dst_ref=here, send_sem=send.at[it, g, o], recv_sem=recv.at[it, g, me],
            device_id=(row, jnp.where(x_now, x_col, y_col)), device_id_type=MESH)

    def row_arrived(it, g, which):
        buffer, recv = (r.first, r.first_recv) if which == 0 else (r.second, r.second_recv)
        _, me = place_of(g, which)
        for o in range(1, side):
            slot = lax.rem(me + o, side)
            here = buffer.at[it, slot, pl.ds(g * chunks, chunks)]
            pltpu.make_async_copy(here, here, recv.at[it, g, slot]).wait()

    def row_merged(it, g, which):
        buffer = r.first if which == 0 else r.second
        return merged_logs([buffer[it, d, pl.ds(g * chunks, chunks)] for d in range(side)])

    def pair_copy(it):
        return pltpu.make_async_remote_copy(
            src_ref=r.stage.at[it], dst_ref=r.pair.at[it, my_core],
            send_sem=r.pair_send.at[it], recv_sem=r.pair_recv.at[it],
            device_id=sibling, device_id_type=MESH)

    def ring_copy(it, o):
        here = r.ring.at[it, my_z]
        return pltpu.make_async_remote_copy(
            src_ref=here, dst_ref=here, send_sem=r.ring_send.at[it, o], recv_sem=r.ring_recv.at[it, my_z],
            device_id=on_z(o), device_id_type=MESH)

    def back_copy(it):
        here = r.gall.at[it, my_core]
        return pltpu.make_async_remote_copy(
            src_ref=here, dst_ref=here, send_sem=r.back_send.at[it], recv_sem=r.back_recv.at[it],
            device_id=sibling, device_id_type=MESH)

    tgt_copy.wait()
    pl.loop(0, r.tgt.shape[0] // 4)(lambda o: start_columns(r, o))

    for it in range(ITERS):
        @pl.loop(0, GROUPS)
        def _(g):
            if it == 0:
                src_copy(g).wait()
            _, me = place_of(g, 0)

            def place(c, value):
                r.first[it, me, c] = value

            row_group(r, it, g, chunks, place)
            if it == 0:
                @pl.when(g == 0)
                def _():
                    pl.semaphore_wait(barrier, 2 * (side - 1) + depth)

            for o in range(1, side):
                row_copy(it, g, 0, o).start()

        if it == 0:
            pl.loop(0, GROUPS // 2)(lambda g: make_group(r, g, chunks))

        @pl.loop(0, GROUPS)
        def _(g):
            row_arrived(it, g, 0)
            _, me = place_of(g, 1)
            r.second[it, me, pl.ds(g * chunks, chunks)] = row_merged(it, g, 0)
            for o in range(1, side):
                row_copy(it, g, 1, o).start()

        if it == 0:
            pl.loop(GROUPS // 2, GROUPS)(lambda g: make_group(r, g, chunks))

        @pl.loop(0, GROUPS)
        def _(g):
            row_arrived(it, g, 1)
            here = pl.ds(g * chunks, chunks)
            r.fall[here] = r.ls[here] * LOG2E - row_merged(it, g, 1)
            col_group(r, g, chunks)

        @pl.loop(0, half)
        def _(j):
            r.stage[it, j] = merge_columns(r, other * half + j)

        pair_copy(it).start()

        @pl.loop(0, half)
        def _(j):
            r.pair[it, my_core, j] = merge_columns(r, my_core * half + j)

        pair_copy(it).wait_recv()
        r.ring[it, my_z] = merged_logs([r.pair[it, 0], r.pair[it, 1]])
        far_first = sorted(range(1, depth), key=lambda o: -min(o, depth - o))
        for o in far_first:
            ring_copy(it, o).start()

        if it == 0:
            @pl.loop(0, n_col)
            def _(c):
                for t in range(TILES):
                    across = norms_across(r.src[TILES * c + t])
                    for h in range(2):
                        r.rnorm[c, pl.ds(2 * t + h, 1), :] = across[:, h * 128:(h + 1) * 128]

            @pl.loop(0, 2 * half)
            def _(c):
                for t in range(TILES):
                    across = norms_across(r.tgt[TILES * c + t])
                    for h in range(2):
                        r.cnorm[c, pl.ds(2 * t + h, 1), :] = across[:, h * 128:(h + 1) * 128]

        if it == ITERS - 1:
            r.f_out[...] = r.fall[...] * (1.0 / SCALE) + r.rnorm[...]

        @pl.loop(0, GROUPS)
        def _(g):
            for o in range(1, side):
                row_copy(it, g, 0, o).wait_send()
                row_copy(it, g, 1, o).wait_send()

        pair_copy(it).wait_send()

        for o in far_first:
            slot = lax.rem(my_z + o, depth)
            here = r.ring.at[it, slot]
            pltpu.make_async_copy(here, here, r.ring_recv.at[it, slot]).wait()
        r.gall[it, my_core] = (
            r.lt[pl.ds(my_core * half, half)] * LOG2E - merged_logs([r.ring[it, d] for d in range(depth)]))
        back_copy(it).start()

        def finish(core):
            if it < ITERS - 1:
                pl.loop(0, half)(lambda j: spread_columns(r, core * half + j, r.gall[it, core, j]))
            else:
                here = pl.ds(core * half, half)
                r.g_out[here] = r.gall[it, core] * (1.0 / SCALE) + r.cnorm[here]

        finish(my_core)
        for o in far_first:
            ring_copy(it, o).wait_send()
        back_copy(it).wait()
        finish(other)


def on_device(n_row, n_col, source, target, log_source, log_target, support, counts):
    row_count = support.shape[0]
    embed = source.shape[1]
    col_count = target.shape[0] // BS
    side = math.isqrt(n_col)
    depth = n_row // 2
    f32 = jnp.float32
    smem = pl.BlockSpec(memory_space=pltpu.SMEM)
    vmem = pl.BlockSpec(memory_space=pltpu.VMEM)
    hbm = pl.BlockSpec(memory_space=pl.ANY)
    dma = pltpu.SemaphoreType.DMA
    row_shape, col_shape = (row_count // TILES, 8, 128), (col_count // TILES, 8, 128)
    half_shape = (col_count // TILES // 2, 8, 128)
    gathered = TILES * 16 * row_count // (TILES * GROUPS)
    f, g = pl.pallas_call(
        functools.partial(kernel, n_row, n_col),
        out_shape=(jax.ShapeDtypeStruct(row_shape, f32), jax.ShapeDtypeStruct(col_shape, f32)),
        in_specs=[smem, smem, hbm, hbm, vmem, vmem],
        out_specs=(vmem, vmem),
        scratch_shapes=[
            pltpu.VMEM((row_count, BS, embed), jnp.bfloat16),
            pltpu.VMEM((col_count, BS, embed), jnp.bfloat16),
            pltpu.VMEM((row_count, BS, BS), f32),
            pltpu.VMEM((row_count, BS, BS), f32),
            pltpu.VMEM((col_count, BS, 128), f32),
            pltpu.VMEM((gathered, 128), f32),
            pltpu.VMEM((gathered, 128), f32),
            pltpu.VMEM(row_shape, jnp.int32),
            pltpu.VMEM(row_shape, f32),
            pltpu.VMEM(row_shape, f32),
            pltpu.VMEM(row_shape, f32),
            pltpu.VMEM(col_shape, f32),
            pltpu.VMEM((ITERS, side) + row_shape, f32),
            pltpu.VMEM((ITERS, side) + row_shape, f32),
            pltpu.VMEM((ITERS,) + half_shape, f32),
            pltpu.VMEM((ITERS, 2) + half_shape, f32),
            pltpu.VMEM((ITERS, depth) + half_shape, f32),
            pltpu.VMEM((ITERS, 2) + half_shape, f32),
            dma(()),
            dma((GROUPS,)),
            dma((ITERS, GROUPS, side)), dma((ITERS, GROUPS, side)),
            dma((ITERS, GROUPS, side)), dma((ITERS, GROUPS, side)),
            dma((ITERS,)), dma((ITERS,)),
            dma((ITERS, depth)), dma((ITERS, depth)),
            dma((ITERS,)), dma((ITERS,)),
        ],
        compiler_params=pltpu.CompilerParams(
            collective_id=0, has_side_effects=True, vmem_limit_bytes=56 * 1024 * 1024),
    )(
        support.T, counts.T,
        source.reshape(row_count, BS, embed), target.reshape(col_count, BS, embed),
        log_source.reshape(row_shape), log_target.reshape(col_shape),
    )
    return f.reshape(-1), g.reshape(-1)


def solution(mesh):
    placed = (P("row", None), P("col", None), P("row"), P("col"), P("row", "col"), P("row", "col"))
    body = functools.partial(on_device, mesh.shape["row"], mesh.shape["col"])
    return jax.shard_map(
        body, mesh=mesh, in_specs=placed, out_specs=(P("row"), P("col")), check_vma=False
    )
```

time: 394 us -> 62.2 us (0.16)
  waiting for transfers between devices: 191 us -> 0 us
  other arithmetic: 87.4 us -> 0 us
  blocking collectives: 74.7 us -> 0 us
  Pallas kernels: 0 us -> 58.5 us
  between operations: 14 us -> 0.64 us
  matrix products: 10 us -> 0 us
  local copies, waits for them, and re-layouts: 12.7 us -> 2.85 us
    all_gather x4 -> x0, waiting for transfers between devices: 190 us -> none  [merged(): everything = jax.tree.map(lambda part: lax.all_gather(part, axis), array)]
    all_gather x4 -> x0, blocking collectives: 74.7 us -> none  [merged(): everything = jax.tree.map(lambda part: lax.all_gather(part, axis), array)]
    pallas_call x0 -> x1, Pallas kernels: none -> 58.5 us  [on_device(): pl.pallas_call(functools.partial(kernel, n_row, n_col), out_shape=(jax.Sh...]
    reduce_sum x6 -> x0, other arithmetic: 38.3 us -> none  [the longest x2 16.7 us: on_device(): jnp.sum(jnp.where(mask_tiles, jnp.exp(scores - local_peak[:, None, :, Non...]
    add x60 -> x0, other arithmetic: 29.1 us -> none  [combine_pairs(): former[1] * jnp.exp(former[0] - peak)]
    reduce_max x5 -> x0, other arithmetic: 18.4 us -> none  [the longest x2 11.4 us: on_device(): block_peak = jnp.max(col_scores, axis=2)]
    dot_general x3 -> x0, matrix products: 10 us -> none  [the longest x1 9.48 us: on_device(): jnp.einsum('rbe,rkce->rkbc', source_blocks, picked, preferred_element_typ...]
    gather x6 -> x0, local copies, waits for them, and re-layouts: 7.92 us -> none  [the longest x1 4.65 us: on_device(): picked = target_blocks[local_block]]
  transfers between devices with their start and end apart: 4 -> 0, of which waited for: 4 -> 0; matrix products, arithmetic and copies ran while one was open for 0% -> 0% of each run, Pallas kernels for 0% -> 0%
where the time goes in v2:
time: 62.2 us; the launch traced here: 62 us
  Pallas kernels  58.5 us (94%)
  local copies, waits for them, and re-layouts  2.85 us (5%)
  between operations  0.64 us (1%)
    pallas_call x1, Pallas kernels, on_device(): pl.pallas_call(functools.partial(kernel, n_row, n_col), out_shape=(jax.Sh...  58.5 us
    unnamed x2, local copies, waits for them, and re-layouts  2.85 us

profile of v2, /device:TPU:1, one launch (start us, length us, event | category | flops | bytes accessed | tf_op | source)
XLA Modules:
  0.0 62.0 jit_solution(381014533503476722)
XLA Ops:
  0.6 58.5 %shard_map.77 = (f32[16,8,128]{2,1,0:T(8,128)}, f32[8,8,128]{2,1,0:T(8,128)}) custom-call(s32[1,64]{1,0:T(1,128)} %bitcast.14, s32[1,64]{1,0:T(1,128)} %bitcast.15, bf16[64,256,128]{2,1,0:T(8,128)(2,1)} %bitcast.8, bf16[32,256,128]{2,1,0:T(8,128)(2,1)} %bitcast.9, f32[16,8,128]{2,1,0:T(8,128)} %bitcast.10, f32[8,8,128]{2,1,0:T(8,128)} %bitcast.12), custom_call_target="tpu_custom_call" | custom-call | tf_op jit(solution)/shard_map/pallas_call | solution.py:381
  59.2 1.5 %copy.10 = f32[16384]{0:T(1024)} copy(f32[16384]{0:T(1024)} %bitcast.11) | data formatting | bytes 131072
  60.6 1.4 %copy.11 = f32[8192]{0:T(1024)} copy(f32[8192]{0:T(1024)} %bitcast.13) | data formatting | bytes 65536

commit v3 on v2

--- a/solution.py
+++ b/solution.py
@@ -17,6 +17,7 @@
 MESH = pl.DeviceIdType.MESH
 TILES = 4
 GROUPS = 4
+TGT_PARTS = 2
 PART = 64
 
 
@@ -82,11 +83,11 @@
     return jnp.clip(r.sup[0, i] - r.first_block, 0, r.tgt.shape[0] - 1)
 
 
-def start_columns(r, o):
-    for a in range(4):
-        block = r.tgt[4 * o + a]
+def start_columns(r, o, count):
+    for a in range(count):
+        block = r.tgt[count * o + a]
         down = jnp.sum(squares(block), axis=1, keepdims=True) * (-SCALE / block.shape[1])
-        r.gcol[4 * o + a] = jnp.broadcast_to(down, (BS, 128))
+        r.gcol[count * o + a] = jnp.broadcast_to(down, (BS, 128))
 
 
 def row_group(r, it, g, chunks, place):
@@ -185,8 +186,14 @@
     chunks = n_col // GROUPS
     half = r.gall.shape[2]
 
-    tgt_copy = pltpu.make_async_copy(r.tgt_hbm, r.tgt, r.tgt_sem)
-    tgt_copy.start()
+    tgt_part = r.tgt.shape[0] // TGT_PARTS
+
+    def tgt_copy(o):
+        here = pl.ds(o * tgt_part, tgt_part)
+        return pltpu.make_async_copy(r.tgt_hbm.at[here], r.tgt.at[here], r.tgt_sem.at[o])
+
+    for o in range(TGT_PARTS):
+        tgt_copy(o).start()
 
     def src_copy(g):
         here = pl.ds(g * chunks * TILES, chunks * TILES)
@@ -257,8 +264,10 @@
             src_ref=here, dst_ref=here, send_sem=r.back_send.at[it], recv_sem=r.back_recv.at[it],
             device_id=sibling, device_id_type=MESH)
 
-    tgt_copy.wait()
-    pl.loop(0, r.tgt.shape[0] // 4)(lambda o: start_columns(r, o))
+    @pl.loop(0, TGT_PARTS)
+    def _(o):
+        tgt_copy(o).wait()
+        start_columns(r, o, tgt_part)
 
     for it in range(ITERS):
         @pl.loop(0, GROUPS)
@@ -278,9 +287,6 @@
 
             for o in range(1, side):
                 row_copy(it, g, 0, o).start()
-
-        if it == 0:
-            pl.loop(0, GROUPS // 2)(lambda g: make_group(r, g, chunks))
 
         @pl.loop(0, GROUPS)
         def _(g):
@@ -289,9 +295,8 @@
             r.second[it, me, pl.ds(g * chunks, chunks)] = row_merged(it, g, 0)
             for o in range(1, side):
                 row_copy(it, g, 1, o).start()
-
-        if it == 0:
-            pl.loop(GROUPS // 2, GROUPS)(lambda g: make_group(r, g, chunks))
+            if it == 0:
+                make_group(r, g, chunks)
 
         @pl.loop(0, GROUPS)
         def _(g):
@@ -352,7 +357,8 @@
 
         def finish(core):
             if it < ITERS - 1:
-                pl.loop(0, half)(lambda j: spread_columns(r, core * half + j, r.gall[it, core, j]))
+                for j in range(half):
+                    spread_columns(r, core * half + j, r.gall[it, core, j])
             else:
                 here = pl.ds(core * half, half)
                 r.g_out[here] = r.gall[it, core] * (1.0 / SCALE) + r.cnorm[here]
@@ -362,6 +368,11 @@
             ring_copy(it, o).wait_send()
         back_copy(it).wait()
         finish(other)
+
+
+def handed_on(f_from, g_from, f_to, g_to):
+    f_to[...] = f_from[...]
+    g_to[...] = g_from[...]
 
 
 def on_device(n_row, n_col, source, target, log_source, log_target, support, counts):
@@ -402,7 +413,7 @@
             pltpu.VMEM((ITERS, 2) + half_shape, f32),
             pltpu.VMEM((ITERS, depth) + half_shape, f32),
             pltpu.VMEM((ITERS, 2) + half_shape, f32),
-            dma(()),
+            dma((TGT_PARTS,)),
             dma((GROUPS,)),
             dma((ITERS, GROUPS, side)), dma((ITERS, GROUPS, side)),
             dma((ITERS, GROUPS, side)), dma((ITERS, GROUPS, side)),
@@ -417,6 +428,12 @@
         source.reshape(row_count, BS, embed), target.reshape(col_count, BS, embed),
         log_source.reshape(row_shape), log_target.reshape(col_shape),
     )
+    f, g = pl.pallas_call(
+        handed_on,
+        out_shape=(jax.ShapeDtypeStruct(row_shape, f32), jax.ShapeDtypeStruct(col_shape, f32)),
+        in_specs=[vmem, vmem],
+        out_specs=(vmem, vmem),
+    )(f, g)
     return f.reshape(-1), g.reshape(-1)
 
 

time: 62.2 us -> 58.8 us (0.945)
  local copies, waits for them, and re-layouts: 2.85 us -> 0 us
    unnamed x2 -> x0, local copies, waits for them, and re-layouts: 2.85 us -> none
    pallas_call x1, Pallas kernels: 58.5 us -> 56.6 us  [on_device(): pl.pallas_call(functools.partial(kernel, n_row, n_col), out_shape=(jax.Sh...]
    pallas_call x0 -> x1, Pallas kernels: none -> 1.48 us  [on_device(): pl.pallas_call(handed_on, out_shape=(jax.ShapeDtypeStruct(row_shape, f32)...]
where the time goes in v3:
time: 58.8 us; the launch traced here: 58.7 us
  Pallas kernels  58 us (99%)
  between operations  0.64 us (1%)
    pallas_call x1, Pallas kernels, on_device(): pl.pallas_call(functools.partial(kernel, n_row, n_col), out_shape=(jax.Sh...  56.6 us
    pallas_call x1, Pallas kernels, on_device(): pl.pallas_call(handed_on, out_shape=(jax.ShapeDtypeStruct(row_shape, f32)...  1.48 us

profile of v3, /device:TPU:1, one launch (start us, length us, event | category | flops | bytes accessed | tf_op | source)
XLA Modules:
  0.0 58.7 jit_solution(353551220857487343)
XLA Ops:
  0.6 56.6 %shard_map.77 = (f32[16,8,128]{2,1,0:T(8,128)}, f32[8,8,128]{2,1,0:T(8,128)}) custom-call(s32[1,64]{1,0:T(1,128)} %bitcast.12, s32[1,64]{1,0:T(1,128)} %bitcast.13, bf16[64,256,128]{2,1,0:T(8,128)(2,1)} %bitcast.8, bf16[32,256,128]{2,1,0:T(8,128)(2,1)} %bitcast.9, f32[16,8,128]{2,1,0:T(8,128)} %bitcast.10, f32[8,8,128]{2,1,0:T(8,128)} %bitcast.11), custom_call_target="tpu_custom_call" | custom-call | tf_op jit(solution)/shard_map/pallas_call | solution.py:392
  57.2 1.5 %shard_map.78 = (f32[16,8,128]{2,1,0:T(8,128)}, f32[8,8,128]{2,1,0:T(8,128)}) custom-call(f32[16,8,128]{2,1,0:T(8,128)} %get-tuple-element.6.f_from, f32[8,8,128]{2,1,0:T(8,128)} %get-tuple-element.7.g_from), custom_call_target="tpu_custom_call" | custom-call | tf_op jit(solution)/shard_map/pallas_call | solution.py:431

commit v4 on v3

--- a/solution.py
+++ b/solution.py
@@ -77,6 +77,14 @@
     low = (square - high.astype(jnp.float32)).astype(jnp.bfloat16)
     ones = jnp.ones((8, block.shape[1]), jnp.bfloat16)
     return ((dot_nt(ones, high) + dot_nt(ones, low)) * (1.0 / block.shape[1]))[0:1]
+
+
+def norm_chunks(blocks, norms, first):
+    for c in (first, first + 1):
+        for t in range(TILES):
+            across = norms_across(blocks[TILES * c + t])
+            for h in range(2):
+                norms[c, pl.ds(2 * t + h, 1), :] = across[:, h * 128:(h + 1) * 128]
 
 
 def block_of(r, i):
@@ -322,21 +330,10 @@
             ring_copy(it, o).start()
 
         if it == 0:
-            @pl.loop(0, n_col)
-            def _(c):
-                for t in range(TILES):
-                    across = norms_across(r.src[TILES * c + t])
-                    for h in range(2):
-                        r.rnorm[c, pl.ds(2 * t + h, 1), :] = across[:, h * 128:(h + 1) * 128]
-
-            @pl.loop(0, 2 * half)
-            def _(c):
-                for t in range(TILES):
-                    across = norms_across(r.tgt[TILES * c + t])
-                    for h in range(2):
-                        r.cnorm[c, pl.ds(2 * t + h, 1), :] = across[:, h * 128:(h + 1) * 128]
+            pl.loop(0, half)(lambda c: norm_chunks(r.tgt, r.cnorm, 2 * c))
 
         if it == ITERS - 1:
+            pl.loop(0, n_col // 2)(lambda c: norm_chunks(r.src, r.rnorm, 2 * c))
             r.f_out[...] = r.fall[...] * (1.0 / SCALE) + r.rnorm[...]
 
         @pl.loop(0, GROUPS)

time: 58.8 us -> 56.9 us (0.968)
  Pallas kernels: 58 us -> 56.1 us
    pallas_call x1, Pallas kernels: 56.6 us -> 54.6 us  [on_device(): pl.pallas_call(functools.partial(kernel, n_row, n_col), out_shape=(jax.Sh...]
where the time goes in v4:
time: 56.9 us; the launch traced here: 56.7 us
  Pallas kernels  56.1 us (99%)
  between operations  0.64 us (1%)
    pallas_call x1, Pallas kernels, on_device(): pl.pallas_call(functools.partial(kernel, n_row, n_col), out_shape=(jax.Sh...  54.6 us
    pallas_call x1, Pallas kernels, on_device(): pl.pallas_call(handed_on, out_shape=(jax.ShapeDtypeStruct(row_shape, f32)...  1.48 us

profile of v4, /device:TPU:1, one launch (start us, length us, event | category | flops | bytes accessed | tf_op | source)
XLA Modules:
  0.0 56.7 jit_solution(17310963555276050326)
XLA Ops:
  0.6 54.6 %shard_map.77 = (f32[16,8,128]{2,1,0:T(8,128)}, f32[8,8,128]{2,1,0:T(8,128)}) custom-call(s32[1,64]{1,0:T(1,128)} %bitcast.12, s32[1,64]{1,0:T(1,128)} %bitcast.13, bf16[64,256,128]{2,1,0:T(8,128)(2,1)} %bitcast.8, bf16[32,256,128]{2,1,0:T(8,128)(2,1)} %bitcast.9, f32[16,8,128]{2,1,0:T(8,128)} %bitcast.10, f32[8,8,128]{2,1,0:T(8,128)} %bitcast.11), custom_call_target="tpu_custom_call" | custom-call | tf_op jit(solution)/shard_map/pallas_call | solution.py:389
  55.2 1.5 %shard_map.78 = (f32[16,8,128]{2,1,0:T(8,128)}, f32[8,8,128]{2,1,0:T(8,128)}) custom-call(f32[16,8,128]{2,1,0:T(8,128)} %get-tuple-element.6.f_from, f32[8,8,128]{2,1,0:T(8,128)} %get-tuple-element.7.g_from), custom_call_target="tpu_custom_call" | custom-call | tf_op jit(solution)/shard_map/pallas_call | solution.py:428

commit v5 on v4

--- a/solution.py
+++ b/solution.py
@@ -153,14 +153,15 @@
         r.lpart[c] = log_sum(sublane_pairs(r.peaks.at[at], r.sums.at[at], 8, 8))
 
 
-def merge_columns(r, chunk):
+def merge_columns(r, chunk, slot):
     for u in range(4):
         mine = jnp.where(r.key[...] == 4 * chunk + u, r.lpart[...], floor_value)
         peak = jnp.max(mine, axis=0)
-        here = pl.ds(8 * u, 8)
+        here = pl.ds(32 * slot + 8 * u, 8)
         r.peaks[here, :] = peak
         r.sums[here, :] = jnp.sum(jnp.exp2(mine - peak[None]), axis=0)
-    return log_sum(sublane_pairs(r.peaks, r.sums, 8, 4))
+    at = pl.ds(32 * slot, 32)
+    return log_sum(sublane_pairs(r.peaks.at[at], r.sums.at[at], 8, 4))
 
 
 def spread_columns(r, chunk, rows):
@@ -169,10 +170,11 @@
 
 
 REFS = (
-    "sup", "cnt", "src_hbm", "tgt_hbm", "ls", "lt", "f_out", "g_out", "src", "tgt", "dots_qp", "dots_pq",
-    "gcol", "peaks", "sums", "key", "fall", "lpart", "rnorm", "cnorm", "first", "second", "stage", "pair",
-    "ring", "gall", "tgt_sem", "src_sem", "first_send", "first_recv", "second_send", "second_recv",
-    "pair_send", "pair_recv", "ring_send", "ring_recv", "back_send", "back_recv",
+    "sup_hbm", "cnt_hbm", "src_hbm", "tgt_hbm", "ls_hbm", "lt_hbm", "f_out", "g_out", "sup", "cnt", "ls",
+    "lt", "src", "tgt", "dots_qp", "dots_pq", "gcol", "peaks", "sums", "key", "fall", "lpart", "rnorm",
+    "cnorm", "first", "second", "stage", "pair", "ring", "gall", "tgt_sem", "src_sem", "slot_sem",
+    "weight_sem", "first_send", "first_recv", "second_send", "second_recv", "pair_send", "pair_recv",
+    "ring_send", "ring_recv", "back_send", "back_recv",
 )
 
 
@@ -203,12 +205,24 @@
     for o in range(TGT_PARTS):
         tgt_copy(o).start()
 
+    slot_copies = [
+        pltpu.make_async_copy(r.sup_hbm, r.sup, r.slot_sem.at[0]),
+        pltpu.make_async_copy(r.cnt_hbm, r.cnt, r.slot_sem.at[1])]
+    for copy in slot_copies:
+        copy.start()
+
     def src_copy(g):
         here = pl.ds(g * chunks * TILES, chunks * TILES)
         return pltpu.make_async_copy(r.src_hbm.at[here], r.src.at[here], r.src_sem.at[g])
 
     for g in range(GROUPS):
         src_copy(g).start()
+
+    weight_copies = [
+        pltpu.make_async_copy(r.ls_hbm, r.ls, r.weight_sem.at[0]),
+        pltpu.make_async_copy(r.lt_hbm, r.lt, r.weight_sem.at[1])]
+    for copy in weight_copies:
+        copy.start()
 
     def on_x(o):
         return (my_row, lax.rem(my_x + o, side) * side + my_y)
@@ -277,6 +291,9 @@
         tgt_copy(o).wait()
         start_columns(r, o, tgt_part)
 
+    for copy in slot_copies:
+        copy.wait()
+
     for it in range(ITERS):
         @pl.loop(0, GROUPS)
         def _(g):
@@ -298,6 +315,12 @@
 
         @pl.loop(0, GROUPS)
         def _(g):
+            if it == 0:
+                @pl.when(g == 0)
+                def _():
+                    for copy in weight_copies:
+                        copy.wait()
+
             row_arrived(it, g, 0)
             _, me = place_of(g, 1)
             r.second[it, me, pl.ds(g * chunks, chunks)] = row_merged(it, g, 0)
@@ -313,15 +336,13 @@
             r.fall[here] = r.ls[here] * LOG2E - row_merged(it, g, 1)
             col_group(r, g, chunks)
 
-        @pl.loop(0, half)
-        def _(j):
-            r.stage[it, j] = merge_columns(r, other * half + j)
+        for j in range(half):
+            r.stage[it, j] = merge_columns(r, other * half + j, j)
 
         pair_copy(it).start()
 
-        @pl.loop(0, half)
-        def _(j):
-            r.pair[it, my_core, j] = merge_columns(r, my_core * half + j)
+        for j in range(half):
+            r.pair[it, my_core, j] = merge_columns(r, my_core * half + j, j)
 
         pair_copy(it).wait_recv()
         r.ring[it, my_z] = merged_logs([r.pair[it, 0], r.pair[it, 1]])
@@ -379,7 +400,6 @@
     side = math.isqrt(n_col)
     depth = n_row // 2
     f32 = jnp.float32
-    smem = pl.BlockSpec(memory_space=pltpu.SMEM)
     vmem = pl.BlockSpec(memory_space=pltpu.VMEM)
     hbm = pl.BlockSpec(memory_space=pl.ANY)
     dma = pltpu.SemaphoreType.DMA
@@ -389,9 +409,13 @@
     f, g = pl.pallas_call(
         functools.partial(kernel, n_row, n_col),
         out_shape=(jax.ShapeDtypeStruct(row_shape, f32), jax.ShapeDtypeStruct(col_shape, f32)),
-        in_specs=[smem, smem, hbm, hbm, vmem, vmem],
+        in_specs=[hbm] * 6,
         out_specs=(vmem, vmem),
         scratch_shapes=[
+            pltpu.SMEM((1, row_count), jnp.int32),
+            pltpu.SMEM((1, row_count), jnp.int32),
+            pltpu.VMEM(row_shape, f32),
+            pltpu.VMEM(col_shape, f32),
             pltpu.VMEM((row_count, BS, embed), jnp.bfloat16),
             pltpu.VMEM((col_count, BS, embed), jnp.bfloat16),
             pltpu.VMEM((row_count, BS, BS), f32),
@@ -412,6 +436,8 @@
             pltpu.VMEM((ITERS, 2) + half_shape, f32),
             dma((TGT_PARTS,)),
             dma((GROUPS,)),
+            dma((2,)),
+            dma((2,)),
             dma((ITERS, GROUPS, side)), dma((ITERS, GROUPS, side)),
             dma((ITERS, GROUPS, side)), dma((ITERS, GROUPS, side)),
             dma((ITERS,)), dma((ITERS,)),

time: 56.9 us -> 55.3 us (0.972)
  Pallas kernels: 56.1 us -> 54.6 us
    pallas_call x1, Pallas kernels: 54.6 us -> 53.1 us  [on_device(): pl.pallas_call(functools.partial(kernel, n_row, n_col), out_shape=(jax.Sh...]
where the time goes in v5:
time: 55.3 us; the launch traced here: 55.2 us
  Pallas kernels  54.6 us (99%)
  between operations  0.64 us (1%)
    pallas_call x1, Pallas kernels, on_device(): pl.pallas_call(functools.partial(kernel, n_row, n_col), out_shape=(jax.Sh...  53.1 us
    pallas_call x1, Pallas kernels, on_device(): pl.pallas_call(handed_on, out_shape=(jax.ShapeDtypeStruct(row_shape, f32)...  1.48 us

profile of v5, /device:TPU:1, one launch (start us, length us, event | category | flops | bytes accessed | tf_op | source)
XLA Modules:
  0.0 55.2 jit_solution(64511499881608968)
XLA Ops:
  0.6 53.1 %shard_map.77 = (f32[16,8,128]{2,1,0:T(8,128)}, f32[8,8,128]{2,1,0:T(8,128)}) custom-call(s32[1,64]{1,0:T(1,128)} %bitcast.12, s32[1,64]{1,0:T(1,128)} %bitcast.13, bf16[64,256,128]{2,1,0:T(8,128)(2,1)} %bitcast.8, bf16[32,256,128]{2,1,0:T(8,128)(2,1)} %bitcast.9, f32[16,8,128]{2,1,0:T(8,128)} %bitcast.10, f32[8,8,128]{2,1,0:T(8,128)} %bitcast.11), custom_call_target="tpu_custom_call" | custom-call | tf_op jit(solution)/shard_map/pallas_call | solution.py:409
  53.7 1.5 %shard_map.78 = (f32[16,8,128]{2,1,0:T(8,128)}, f32[8,8,128]{2,1,0:T(8,128)}) custom-call(f32[16,8,128]{2,1,0:T(8,128)} %get-tuple-element.6.f_from, f32[8,8,128]{2,1,0:T(8,128)} %get-tuple-element.7.g_from), custom_call_target="tpu_custom_call" | custom-call | tf_op jit(solution)/shard_map/pallas_call | solution.py:454

commit v6 on v5

--- a/solution.py
+++ b/solution.py
@@ -108,13 +108,18 @@
             if it == 0:
                 made = dot_nt(r.tgt[block], r.src[i]) * (2.0 * SCALE / r.src.shape[2])
                 r.dots_qp[i] = made
+            else:
+                held = r.gall.at[it - 1, block // (4 * r.half), lax.rem(block // 4, r.half)]
+                down = [lane_column(held[pl.ds(2 * lax.rem(block, 4) + h, 1), :]) for h in range(2)]
             for h in range(2):
                 lanes = slice(h * 128, (h + 1) * 128)
                 if it == 0:
                     products = lambda k: made[k:k + PART, lanes]
+                    offsets = lambda k: r.gcol[block, k:k + PART, :]
                 else:
                     products = lambda k: r.dots_qp[i, k:k + PART, lanes]
-                peak, total = tile_pairs(products, lambda k: r.gcol[block, k:k + PART, :])
+                    offsets = lambda k: down[k // 128][k % 128:k % 128 + PART]
+                peak, total = tile_pairs(products, offsets)
                 here = pl.ds(64 * k + 8 * (2 * t + h), 8)
                 r.peaks[here, :] = peak + dead
                 r.sums[here, :] = total
@@ -164,11 +169,6 @@
     return log_sum(sublane_pairs(r.peaks.at[at], r.sums.at[at], 8, 4))
 
 
-def spread_columns(r, chunk, rows):
-    for j in range(8):
-        r.gcol[4 * chunk + j // 2, (j % 2) * 128:(j % 2 + 1) * 128, :] = lane_column(rows[j:j + 1])
-
-
 REFS = (
     "sup_hbm", "cnt_hbm", "src_hbm", "tgt_hbm", "ls_hbm", "lt_hbm", "f_out", "g_out", "sup", "cnt", "ls",
     "lt", "src", "tgt", "dots_qp", "dots_pq", "gcol", "peaks", "sums", "key", "fall", "lpart", "rnorm",
@@ -194,7 +194,7 @@
     other = 1 - my_core
     r.first_block = my_col * r.tgt.shape[0]
     chunks = n_col // GROUPS
-    half = r.gall.shape[2]
+    r.half = half = r.gall.shape[2]
 
     tgt_part = r.tgt.shape[0] // TGT_PARTS
 
@@ -374,10 +374,7 @@
         back_copy(it).start()
 
         def finish(core):
-            if it < ITERS - 1:
-                for j in range(half):
-                    spread_columns(r, core * half + j, r.gall[it, core, j])
-            else:
+            if it == ITERS - 1:
                 here = pl.ds(core * half, half)
                 r.g_out[here] = r.gall[it, core] * (1.0 / SCALE) + r.cnorm[here]
 

time: 55.3 us -> 54.9 us (level)
  no operation moved by 1% of the time
where the time goes in v6:
time: 54.9 us; the launch traced here: 54.8 us
  Pallas kernels  54.2 us (99%)
  between operations  0.64 us (1%)
    pallas_call x1, Pallas kernels, on_device(): pl.pallas_call(functools.partial(kernel, n_row, n_col), out_shape=(jax.Sh...  52.7 us
    pallas_call x1, Pallas kernels, on_device(): pl.pallas_call(handed_on, out_shape=(jax.ShapeDtypeStruct(row_shape, f32)...  1.48 us

profile of v6, /device:TPU:1, one launch (start us, length us, event | category | flops | bytes accessed | tf_op | source)
XLA Modules:
  0.0 54.8 jit_solution(14416082998943536246)
XLA Ops:
  0.6 52.7 %shard_map.77 = (f32[16,8,128]{2,1,0:T(8,128)}, f32[8,8,128]{2,1,0:T(8,128)}) custom-call(s32[1,64]{1,0:T(1,128)} %bitcast.12, s32[1,64]{1,0:T(1,128)} %bitcast.13, bf16[64,256,128]{2,1,0:T(8,128)(2,1)} %bitcast.8, bf16[32,256,128]{2,1,0:T(8,128)(2,1)} %bitcast.9, f32[16,8,128]{2,1,0:T(8,128)} %bitcast.10, f32[8,8,128]{2,1,0:T(8,128)} %bitcast.11), custom_call_target="tpu_custom_call" | custom-call | tf_op jit(solution)/shard_map/pallas_call | solution.py:406
  53.3 1.5 %shard_map.78 = (f32[16,8,128]{2,1,0:T(8,128)}, f32[8,8,128]{2,1,0:T(8,128)}) custom-call(f32[16,8,128]{2,1,0:T(8,128)} %get-tuple-element.6.f_from, f32[8,8,128]{2,1,0:T(8,128)} %get-tuple-element.7.g_from), custom_call_target="tpu_custom_call" | custom-call | tf_op jit(solution)/shard_map/pallas_call | solution.py:451

commit v7 on v6

--- a/solution.py
+++ b/solution.py
@@ -94,8 +94,16 @@
 def start_columns(r, o, count):
     for a in range(count):
         block = r.tgt[count * o + a]
-        down = jnp.sum(squares(block), axis=1, keepdims=True) * (-SCALE / block.shape[1])
-        r.gcol[count * o + a] = jnp.broadcast_to(down, (BS, 128))
+        square = squares(block)
+        if a % 2 == 0:
+            down = jnp.broadcast_to(jnp.sum(square, axis=1, keepdims=True), (BS, 128))
+        else:
+            high = square.astype(jnp.bfloat16)
+            low = (square - high.astype(jnp.float32)).astype(jnp.bfloat16)
+            ones = jnp.ones((block.shape[1], 128), jnp.bfloat16)
+            down = (jnp.dot(high, ones, preferred_element_type=jnp.float32)
+                    + jnp.dot(low, ones, preferred_element_type=jnp.float32))
+        r.gcol[count * o + a] = down * (-SCALE / block.shape[1])
 
 
 def row_group(r, it, g, chunks, place):
@@ -182,6 +190,10 @@
     pass
 
 
+def far_first(ring):
+    return sorted(range(1, ring), key=lambda o: -min(o, ring - o))
+
+
 def kernel(n_row, n_col, *refs):
     r = Refs()
     for name, ref in zip(REFS, refs, strict=True):
@@ -310,7 +322,7 @@
                 def _():
                     pl.semaphore_wait(barrier, 2 * (side - 1) + depth)
 
-            for o in range(1, side):
+            for o in far_first(side):
                 row_copy(it, g, 0, o).start()
 
         @pl.loop(0, GROUPS)
@@ -324,7 +336,7 @@
             row_arrived(it, g, 0)
             _, me = place_of(g, 1)
             r.second[it, me, pl.ds(g * chunks, chunks)] = row_merged(it, g, 0)
-            for o in range(1, side):
+            for o in far_first(side):
                 row_copy(it, g, 1, o).start()
             if it == 0:
                 make_group(r, g, chunks)
@@ -346,8 +358,7 @@
 
         pair_copy(it).wait_recv()
         r.ring[it, my_z] = merged_logs([r.pair[it, 0], r.pair[it, 1]])
-        far_first = sorted(range(1, depth), key=lambda o: -min(o, depth - o))
-        for o in far_first:
+        for o in far_first(depth):
             ring_copy(it, o).start()
 
         if it == 0:
@@ -365,7 +376,7 @@
 
         pair_copy(it).wait_send()
 
-        for o in far_first:
+        for o in far_first(depth):
             slot = lax.rem(my_z + o, depth)
             here = r.ring.at[it, slot]
             pltpu.make_async_copy(here, here, r.ring_recv.at[it, slot]).wait()
@@ -379,7 +390,7 @@
                 r.g_out[here] = r.gall[it, core] * (1.0 / SCALE) + r.cnorm[here]
 
         finish(my_core)
-        for o in far_first:
+        for o in far_first(depth):
             ring_copy(it, o).wait_send()
         back_copy(it).wait()
         finish(other)

time: 54.9 us -> 54.3 us (0.989)
  Pallas kernels: 54.2 us -> 53.5 us
    pallas_call x1, Pallas kernels: 52.7 us -> 52.1 us  [on_device(): pl.pallas_call(functools.partial(kernel, n_row, n_col), out_shape=(jax.Sh...]
where the time goes in v7:
time: 54.3 us; the launch traced here: 54.2 us
  Pallas kernels  53.5 us (99%)
  between operations  0.64 us (1%)
    pallas_call x1, Pallas kernels, on_device(): pl.pallas_call(functools.partial(kernel, n_row, n_col), out_shape=(jax.Sh...  52.1 us
    pallas_call x1, Pallas kernels, on_device(): pl.pallas_call(handed_on, out_shape=(jax.ShapeDtypeStruct(row_shape, f32)...  1.48 us

profile of v7, /device:TPU:1, one launch (start us, length us, event | category | flops | bytes accessed | tf_op | source)
XLA Modules:
  0.0 54.2 jit_solution(17301293036566693889)
XLA Ops:
  0.6 52.1 %shard_map.77 = (f32[16,8,128]{2,1,0:T(8,128)}, f32[8,8,128]{2,1,0:T(8,128)}) custom-call(s32[1,64]{1,0:T(1,128)} %bitcast.12, s32[1,64]{1,0:T(1,128)} %bitcast.13, bf16[64,256,128]{2,1,0:T(8,128)(2,1)} %bitcast.8, bf16[32,256,128]{2,1,0:T(8,128)(2,1)} %bitcast.9, f32[16,8,128]{2,1,0:T(8,128)} %bitcast.10, f32[8,8,128]{2,1,0:T(8,128)} %bitcast.11), custom_call_target="tpu_custom_call" | custom-call | tf_op jit(solution)/shard_map/pallas_call | solution.py:417
  52.7 1.5 %shard_map.78 = (f32[16,8,128]{2,1,0:T(8,128)}, f32[8,8,128]{2,1,0:T(8,128)}) custom-call(f32[16,8,128]{2,1,0:T(8,128)} %get-tuple-element.6.f_from, f32[8,8,128]{2,1,0:T(8,128)} %get-tuple-element.7.g_from), custom_call_target="tpu_custom_call" | custom-call | tf_op jit(solution)/shard_map/pallas_call | solution.py:462
